TPU v7x, 32 devices: a whole 2x2x4 slice. The times are simulated.
32 devices in a mesh: lp: 2 (over y), row: 4 (over z), col: 4 (over x, core).
Axes of the slice: x: 2, y: 2, z: 4, core: 2. Of those that a mesh axis runs over, the one named last changes fastest.
Arguments:
- tile_values: bfloat16 [8, 4, 16, 256, 256], P(('lp', 'row'), 'col'), parts along dimension 0, may hold values from -0.125 to 0.125
- tile_spots: int32 [8, 4, 16, 2], P(('lp', 'row'), 'col'), parts along dimension 0, may hold values from 0 to 3, as said below
- tile_counts: int32 [8, 4], P(('lp', 'row'), 'col'), parts along dimension 0, may hold values from 1 to 16, as said below
- objective: float32 [8192], P(('lp', 'col')), parts along dimension 0, may hold values from -21 to 21
- lower_bound: float32 [8192], P(('lp', 'col')), parts along dimension 0, may hold values from -1.5 to -0.2
- bound_span: float32 [8192], P(('lp', 'col')), parts along dimension 0, may hold values from 0.5 to 2.5
- var_kind: int32 [8192], P(('lp', 'col')), parts along dimension 0, may hold values from 0 to 3
- right_side: float32 [256, 4096], P('lp', 'row'), parts along dimension 0, may hold values from -63 to 63
- row_kind: int32 [8192], P(('lp', 'row')), parts along dimension 0, may hold values 0 or 1
- primal_start: float32 [256, 4096], P('lp', 'col'), parts along dimension 0, may hold values from -4 to 4
- dual_start: float32 [256, 4096], P('lp', 'row'), parts along dimension 0, may hold values from -4 to 4
Outputs:
- primal_iterate: float32 [256, 4096], P('lp', 'col'), parts along dimension 0
- dual_iterate: float32 [256, 4096], P('lp', 'row'), parts along dimension 0
There are 2 independent parts, one for each index of `lp`. A program takes and returns all parts, laid end to end along the dimension named above; each array names one. Nothing has to cross between parts.
Inputs may be any that keep to these rules, and one draw needn't show every extreme that they name: Slot t of grid cell (r, c) names row block tile_spots[r, c, t, 0] below 4 and column block tile_spots[r, c, t, 1] below 4 of that cell; the slots of one cell name distinct pairs. Slots 0 to tile_counts - 1 of a grid cell hold its tiles; some cell uses all 16 slots.
All inputs are finite; a program needn't handle non-finite values. No bound on the sum of `row_kind` on one device may be relied on, other than what follows from the above.
Results may differ from a plain program's by a relative error of at most 0.0014.
Values sent between devices are 32-bit elements; how exact they have to be, the bound alone decides.
A program may use at most 64 MiB of HBM per device.

v0:
```python
import jax
import jax.numpy as jnp
from jax import lax
from jax.sharding import PartitionSpec as P

ITERS = 3


STEP_SCALE = 0.4
EPSILON = 1e-06


def project_primal(values, lower_bound, upper_bound, var_kind):
    low_on = (var_kind == 1) | (var_kind == 3)
    high_on = (var_kind == 2) | (var_kind == 3)
    values = jnp.where(low_on, jnp.maximum(values, lower_bound), values)
    return jnp.where(high_on, jnp.minimum(values, upper_bound), values)


def project_dual(values, row_kind):
    return jnp.where(row_kind == 1, jnp.maximum(values, 0.0), values)


def weight_update(weight, primal_squares, dual_squares, total_cols, total_rows):
    primal_spread = jnp.sqrt(primal_squares / total_cols + EPSILON)
    dual_spread = jnp.sqrt(dual_squares / total_rows + EPSILON)
    return jnp.sqrt(weight * dual_spread / primal_spread)


def pick_matrix(indices, in_use, blocks):
    live_slots = jnp.arange(indices.shape[0]) < in_use
    hits = (indices[:, None] == jnp.arange(blocks)[None, :]) & live_slots[:, None]
    return hits.astype(jnp.float32)


def primal_product(tile_set, places, in_use, extrapolated, row_blocks):
    scenarios = extrapolated.shape[0]
    tile_width = tile_set.shape[-1]
    blocks = extrapolated.reshape(scenarios, -1, tile_width)
    picked = jnp.take(blocks, places[:, 1], axis=1)
    products = jnp.einsum("tij,ktj->kti", tile_set, picked, preferred_element_type=jnp.float32)
    target = pick_matrix(places[:, 0], in_use, row_blocks)
    summed = jnp.einsum("tr,kti->kri", target, products, precision=lax.Precision.HIGHEST)
    return summed.reshape(scenarios, row_blocks * tile_width)


def dual_product(tile_set, places, in_use, dual_half, col_blocks):
    scenarios = dual_half.shape[0]
    tile_width = tile_set.shape[-1]
    blocks = dual_half.reshape(scenarios, -1, tile_width)
    picked = jnp.take(blocks, places[:, 0], axis=1)
    products = jnp.einsum("tij,kti->ktj", tile_set, picked, preferred_element_type=jnp.float32)
    target = pick_matrix(places[:, 1], in_use, col_blocks)
    summed = jnp.einsum("tc,ktj->kcj", target, products, precision=lax.Precision.HIGHEST)
    return summed.reshape(scenarios, col_blocks * tile_width)


def local(
    tile_values,
    tile_spots,
    tile_counts,
    objective,
    lower_bound,
    bound_span,
    var_kind,
    right_side,
    row_kind,
    primal_start,
    dual_start,
):
    tile_set = tile_values.reshape(tile_values.shape[2:])
    places = tile_spots.reshape(tile_spots.shape[2:])
    in_use = tile_counts.reshape(())
    tile_width = tile_set.shape[-1]
    row_blocks = right_side.shape[1] // tile_width
    col_blocks = objective.shape[0] // tile_width
    row_groups = lax.axis_size("row")
    col_groups = lax.axis_size("col")
    total_rows = right_side.shape[1] * row_groups
    total_cols = objective.shape[0] * col_groups
    upper_bound = lower_bound + bound_span
    objective_squares = lax.psum(jnp.sum(objective * objective), "col")
    objective_scale = jnp.sqrt(objective_squares / total_cols + EPSILON)
    side_squares = jnp.sum(right_side * right_side, axis=1)
    side_total = lax.psum(side_squares, "row")
    weight = objective_scale / jnp.sqrt(side_total / total_rows + EPSILON)
    primal, dual_vec = (primal_start, dual_start)
    dual_stat = side_squares
    primal_total = None
    for iteration in range(ITERS):
        final = iteration == ITERS - 1
        dual_half = dual_vec.astype(jnp.bfloat16)
        partial_gradient = dual_product(tile_set, places, in_use, dual_half, col_blocks)
        gradient = lax.psum(partial_gradient, "row")
        primal_step = (STEP_SCALE / weight)[:, None]
        primal_next = project_primal(
            primal - primal_step * (objective - gradient), lower_bound, upper_bound, var_kind
        )
        extrapolated = (2.0 * primal_next - primal).astype(jnp.bfloat16)
        partial_image = primal_product(tile_set, places, in_use, extrapolated, row_blocks)
        primal_squares = jnp.sum((primal_next - primal_start) ** 2, axis=1)
        image = lax.psum(partial_image, "col")
        dual_step = (STEP_SCALE * weight)[:, None]
        dual_next = project_dual(dual_vec + dual_step * (right_side - image), row_kind)
        dual_stat = jnp.sum((dual_next - dual_start) ** 2, axis=1)
        if not final:
            primal_total = lax.psum(primal_squares, "col")
            dual_total = lax.psum(dual_stat, "row")
            weight = weight_update(weight, primal_total, dual_total, total_cols, total_rows)
        primal, dual_vec = (primal_next, dual_next)
    return (primal, dual_vec)


def solution(mesh):
    placed = (
        P(("lp", "row"), "col", None, None, None),
        P(("lp", "row"), "col", None, None),
        P(("lp", "row"), "col"),
        P(("lp", "col")),
        P(("lp", "col")),
        P(("lp", "col")),
        P(("lp", "col")),
        P("lp", "row"),
        P(("lp", "row")),
        P("lp", "col"),
        P("lp", "row"),
    )
    return jax.shard_map(
        local,
        mesh=mesh,
        in_specs=placed,
        out_specs=(P("lp", "col"), P("lp", "row")),
        check_vma=False,
    )
```

profile of v0, /device:TPU:0, one launch (start us, length us, event | category | flops | bytes accessed | tf_op | source)
XLA Modules:
  0.0 304.4 jit_solution(13427075020519906611)
XLA Ops:
  9.5 1.4 multiply_reduce_fusion.5
  10.9 1.2 copy.13
  12.3 1.6 gather_fusion
  13.9 1.7 fusion.24
  15.7 2.0 fusion.42
  17.7 1.0 copy.44
  18.8 8.9 %psum.84 = f32[]{:T(128)} all-reduce(f32[]{:T(128)} %multiply_reduce_fusion.5), channel_id=1, replica_groups=mesh['lp'=2,'row'=4,'col'=4] {'col'}, use_global_device_ids=true, to_apply=%region_1.0 | all-reduce | flops 1 | bytes 8 | tf_op jit(solution)/shard_map/psum | solution.py:82
  28.6 12.0 %psum.85 = f32[128]{0:T(128)S(1)} all-reduce(f32[128]{0:T(128)S(1)} %multiply_reduce_fusion.4), channel_id=1, replica_groups=mesh['lp'=2,'row'=4,'col'=4] {'row'}, use_global_device_ids=true, to_apply=%region_3.0 | all-reduce | flops 128 | bytes 1024 | tf_op jit(solution)/shard_map/psum | solution.py:85
  40.6 1.2 copy.17
  41.9 18.2 %all-reduce.7.cloned.1.call-done = f32[128,1024]{0,1:T(8,128)} async-done(((f32[128,1024]{0,1:T(8,128)}), f32[128,1024]{0,1:T(8,128)}) %all-reduce.7.cloned.1.call-update) | async-done | bytes 524304 | tf_op jit(solution)/shard_map/psum | solution.py:94
  60.1 2.0 multiply_reduce_fusion.2
  62.8 1.1 copy.19
  63.9 1.6 gather_fusion.1
  65.5 2.0 fusion.27
  67.5 2.8 fusion.45
  70.4 2.1 copy.45
  72.5 2.0 copy.22
  74.5 31.2 %all-reduce.9.cloned.1.call-done = f32[128,1024]{0,1:T(8,128)} async-done(((f32[128,1024]{0,1:T(8,128)}), f32[128,1024]{0,1:T(8,128)}) %all-reduce.9.cloned.1.call-update) | async-done | bytes 524304 | tf_op jit(solution)/shard_map/psum | solution.py:102
  105.7 1.6 multiply_reduce_fusion.3
  108.2 1.1 copy.26
  109.3 1.6 gather_fusion.2
  110.9 1.7 fusion.30
  112.7 2.8 fusion.48
  115.5 2.0 copy.46
  117.6 5.8 %psum.89 = f32[128]{0:T(128)S(1)} all-reduce(f32[128]{0:T(128)S(1)} %get-tuple-element.17), channel_id=1, replica_groups=mesh['lp'=2,'row'=4,'col'=4] {'col'}, use_global_device_ids=true, to_apply=%region_9.11 | all-reduce | flops 128 | bytes 1024 | tf_op jit(solution)/shard_map/psum | solution.py:107
  123.4 12.2 %psum.88 = f32[128]{0:T(128)S(1)} all-reduce(f32[128]{0:T(128)S(1)} %get-tuple-element.15), channel_id=1, replica_groups=mesh['lp'=2,'row'=4,'col'=4] {'row'}, use_global_device_ids=true, to_apply=%region_7.9 | all-reduce | flops 128 | bytes 1024 | tf_op jit(solution)/shard_map/psum | solution.py:108
  135.6 20.7 %all-reduce.11.cloned.1.call-done = f32[128,1024]{0,1:T(8,128)} async-done(((f32[128,1024]{0,1:T(8,128)}), f32[128,1024]{0,1:T(8,128)}) %all-reduce.11.cloned.1.call-update) | async-done | bytes 524304 | tf_op jit(solution)/shard_map/psum | solution.py:94
  156.2 2.0 multiply_reduce_fusion
  160.6 2.8 fusion.51
  163.5 2.1 copy.47
  165.6 33.2 %all-reduce.13.cloned.1.call-done = f32[128,1024]{0,1:T(8,128)} async-done(((f32[128,1024]{0,1:T(8,128)}), f32[128,1024]{0,1:T(8,128)}) %all-reduce.13.cloned.1.call-update) | async-done | bytes 524304 | tf_op jit(solution)/shard_map/psum | solution.py:102
  198.9 1.4 multiply_reduce_fusion.1
  201.2 1.6 gather_fusion.4
  202.9 1.7 fusion.36
  204.6 2.8 fusion.54
  207.4 2.0 copy.48
  209.5 5.8 %psum.93 = f32[128]{0:T(128)S(1)} all-reduce(f32[128]{0:T(128)S(1)} %get-tuple-element.11), channel_id=1, replica_groups=mesh['lp'=2,'row'=4,'col'=4] {'col'}, use_global_device_ids=true, to_apply=%region_15.17 | all-reduce | flops 128 | bytes 1024 | tf_op jit(solution)/shard_map/psum | solution.py:107
  215.3 11.8 %psum.92 = f32[128]{0:T(128)S(1)} all-reduce(f32[128]{0:T(128)S(1)} %get-tuple-element.9), channel_id=1, replica_groups=mesh['lp'=2,'row'=4,'col'=4] {'row'}, use_global_device_ids=true, to_apply=%region_13.15 | all-reduce | flops 128 | bytes 1024 | tf_op jit(solution)/shard_map/psum | solution.py:108
  227.2 20.9 %all-reduce.15.cloned.1.call-done = f32[128,1024]{0,1:T(8,128)} async-done(((f32[128,1024]{0,1:T(8,128)}), f32[128,1024]{0,1:T(8,128)}) %all-reduce.15.cloned.1.call-update) | async-done | bytes 524304 | tf_op jit(solution)/shard_map/psum | solution.py:94
  248.1 3.3 %subtract_convert_fusion = (bf16[128,1024]{0,1:T(8,128)(2,1)S(1)}, f32[128,1024]{0,1:T(8,128)}) fusion(f32[128,1024]{0,1:T(8,128)S(1)} %copy-done.5, f32[1024]{0:T(1024)S(1)} %add.59, f32[1024]{0:T(1024)S(1)} %copy-done.10, f32[128,1024]{0,1:T(8,128)} %all-reduce.15.cloned.1.call-done, f32[1024]{0:T(1024)S(1)} %copy-done.11, ...), kind=kLoop, calls=%fused_computation.75 | loop fusion | flops 1310720 | bytes 1849856 | tf_op jit(solution)/shard_map/convert_element_type | solution.py:99
  251.6 1.6 gather_fusion.5
  253.2 2.0 fusion.39
  255.2 2.8 fusion.57
  258.1 2.1 copy.49
  260.1 2.0 copy.42
  262.2 31.3 %all-reduce.17.cloned.1.call-done = f32[128,1024]{0,1:T(8,128)} async-done(((f32[128,1024]{0,1:T(8,128)}), f32[128,1024]{0,1:T(8,128)}) %all-reduce.17.cloned.1.call-update) | async-done | bytes 524304 | tf_op jit(solution)/shard_map/psum | solution.py:102
  293.4 2.1 maximum_select_fusion
  295.5 2.0 copy.43
  (67 shorter events, 7.5 us)
Async XLA Ops:
  7.2 6.8 %copy-start = (bf16[1,1,16,256,256]{4,3,2,1,0:T(8,128)(2,1)S(1)}, bf16[1,1,16,256,256]{4,3,2,1,0:T(8,128)(2,1)}, u32[]{:S(2)}) copy-start(bf16[1,1,16,256,256]{4,3,2,1,0:T(8,128)(2,1)} %param.13) | copy-start | bytes 6291460
  7.2 52.9 %all-reduce.7.cloned.1.call-start = ((), (), s32[]{:S(2)}) async-start(), calls=%async_computation | async-start | bytes 1048576 | tf_op jit(solution)/shard_map/psum | solution.py:94
  12.1 3.6 %copy-start.2 = (f32[128,1024]{0,1:T(8,128)}, f32[128,1024]{0,1:T(8,128)S(1)}, u32[]{:S(2)}) copy-start(f32[128,1024]{0,1:T(8,128)S(1)} %copy.13) | copy-start | bytes 1572868
  15.7 12.8 %copy-start.9 = (f32[128,1024]{1,0:T(8,128)S(1)}, f32[128,1024]{1,0:T(8,128)}, u32[]{:S(2)}) copy-start(f32[128,1024]{1,0:T(8,128)} %param.20) | copy-start | bytes 1572868
  17.7 24.2 %copy-start.10 = (f32[1024]{0:T(1024)S(1)}, f32[1024]{0:T(1024)}, u32[]{:S(2)}) copy-start(f32[1024]{0:T(1024)} %param.17) | copy-start | bytes 12292
  17.7 24.2 %copy-start.12 = (f32[1024]{0:T(1024)S(1)}, f32[1024]{0:T(1024)}, u32[]{:S(2)}) copy-start(f32[1024]{0:T(1024)} %param.18) | copy-start | bytes 12292
  17.7 24.2 %copy-start.14 = (s32[1024]{0:T(1024)S(1)}, s32[1024]{0:T(1024)}, u32[]{:S(2)}) copy-start(s32[1024]{0:T(1024)} %param.19) | copy-start | bytes 12292
  17.7 42.4 %copy-start.11 = (f32[1024]{0:T(1024)S(1)}, f32[1024]{0:T(1024)}, u32[]{:S(2)}) copy-start(f32[1024]{0:T(1024)} %param.16) | copy-start | bytes 12292
  18.8 87.0 %all-reduce.9.cloned.1.call-start = ((), (), s32[]{:S(2)}) async-start(), calls=%async_computation.1 | async-start | bytes 1048576 | tf_op jit(solution)/shard_map/psum | solution.py:102
  67.5 7.0 %copy-start.13 = (s32[1024]{0:T(1024)S(1)}, s32[1024]{0:T(1024)}, u32[]{:S(2)}) copy-start(s32[1024]{0:T(1024)} %param.21) | copy-start | bytes 12292
  72.4 83.8 %all-reduce.11.cloned.1.call-start = ((), (), s32[]{:S(2)}) async-start(), calls=%async_computation.2 | async-start | bytes 1048576 | tf_op jit(solution)/shard_map/psum | solution.py:94
  107.3 0.9 copy-start.6
  117.6 81.3 %all-reduce.13.cloned.1.call-start = ((), (), s32[]{:S(2)}) async-start(), calls=%async_computation.3 | async-start | bytes 1048576 | tf_op jit(solution)/shard_map/psum | solution.py:102
  158.2 0.8 copy-start.4
  160.6 38.2 %copy-start.1 = (f32[128,1024]{0,1:T(8,128)S(1)}, f32[128,1024]{0,1:T(8,128)}, u32[]{:S(2)}) copy-start(f32[128,1024]{0,1:T(8,128)} %copy.22) | copy-start | bytes 1572868
  160.6 38.2 %copy-start.3 = (f32[128,1024]{0,1:T(8,128)S(1)}, f32[128,1024]{0,1:T(8,128)}, u32[]{:S(2)}) copy-start(f32[128,1024]{0,1:T(8,128)} %copy-done.2) | copy-start | bytes 1572868
  165.5 82.5 %all-reduce.15.cloned.1.call-start = ((), (), s32[]{:S(2)}) async-start(), calls=%async_computation.4 | async-start | bytes 1048576 | tf_op jit(solution)/shard_map/psum | solution.py:94
  200.3 0.8 copy-start.7
  204.6 43.5 %copy-start.5 = (f32[128,1024]{0,1:T(8,128)S(1)}, f32[128,1024]{0,1:T(8,128)}, u32[]{:S(2)}) copy-start(f32[128,1024]{0,1:T(8,128)} %copy-done.4) | copy-start | bytes 1572868
  209.5 84.0 %all-reduce.17.cloned.1.call-start = ((), (), s32[]{:S(2)}) async-start(), calls=%async_computation.5 | async-start | bytes 1048576 | tf_op jit(solution)/shard_map/psum | solution.py:102
  255.2 38.2 %copy-start.8 = (f32[128,1024]{0,1:T(8,128)S(1)}, f32[128,1024]{0,1:T(8,128)}, u32[]{:S(2)}) copy-start(f32[128,1024]{0,1:T(8,128)} %copy-done.7) | copy-start | bytes 1572868
Sparse Core Ops, SparseCore 0:
  18.9 41.1 all-reduce.6
  72.6 33.1 all-reduce.8
  117.7 38.4 all-reduce.10
  165.7 33.1 all-reduce.12
  209.6 38.4 all-reduce.14
  260.3 33.1 all-reduce.16
where the time goes:
time: 306 us; the launch traced here: 304 us
  waiting for transfers between devices  156 us (51%)
  blocking collectives  56.4 us (18%)
  local copies, waits for them, and re-layouts  33.8 us (11%)
  matrix products  26.2 us (9%)
  other arithmetic  16.3 us (5%)
  between operations  15.9 us (5%)
    psum x3, waiting for transfers between devices, local(): image = lax.psum(partial_image, 'col')  95.7 us
    psum x3, waiting for transfers between devices, local(): gradient = lax.psum(partial_gradient, 'row')  59.7 us
    psum x2, blocking collectives, local(): dual_total = lax.psum(dual_stat, 'row')  24 us
    psum x1, blocking collectives, local(): side_total = lax.psum(side_squares, 'row')  12 us
    psum x2, blocking collectives, local(): primal_total = lax.psum(primal_squares, 'col')  11.5 us
    unnamed x35, local copies, waits for them, and re-layouts  10.3 us
    psum x1, blocking collectives, local(): objective_squares = lax.psum(jnp.sum(objective * objective), 'col')  8.93 us
    dot_general x3, matrix products, primal_product(): jnp.einsum('tr,kti->kri', target, products, precision=lax.Precision.HIGHEST)  8.48 us
  transfers between devices with their start and end apart: 6, of which 6 were waited for; matrix products, arithmetic and copies ran while one was open for 2% of the time, Pallas kernels for 0%

commit v1 on v0

--- a/solution.py
+++ b/solution.py
@@ -1,13 +1,18 @@
+import functools
+
 import jax
 import jax.numpy as jnp
 from jax import lax
+from jax.experimental import pallas as pl
+from jax.experimental.pallas import tpu as pltpu
 from jax.sharding import PartitionSpec as P
 
 ITERS = 3
-
-
 STEP_SCALE = 0.4
 EPSILON = 1e-06
+SUB = 8
+LANE = 128
+MESH = pl.DeviceIdType.MESH
 
 
 def project_primal(values, lower_bound, upper_bound, var_kind):
@@ -55,7 +60,7 @@
     return summed.reshape(scenarios, col_blocks * tile_width)
 
 
-def local(
+def plain(
     tile_values,
     tile_spots,
     tile_counts,
@@ -111,6 +116,330 @@
     return (primal, dual_vec)
 
 
+def kernel(
+    n_row,
+    n_col,
+    chunks,
+    tiles,
+    spots,
+    counts,
+    objective,
+    lower,
+    span,
+    var_kind,
+    right_side,
+    row_kind,
+    primal_start,
+    dual_start,
+    primal_out,
+    dual_out,
+    matrix,
+    matrix_t,
+    primal_all,
+    dual_all,
+    row_send,
+    col_send,
+    row_recv,
+    col_recv,
+    cost_all,
+    cost_total,
+    row_rs_out,
+    row_rs_in,
+    row_ag_out,
+    row_ag_in,
+    col_rs_out,
+    col_rs_in,
+    col_ag_out,
+    col_ag_in,
+    cost_out,
+    cost_in,
+):
+    r = lax.axis_index("row")
+    c = lax.axis_index("col")
+    slots, width = tiles.shape[0], tiles.shape[1]
+    n_vars = objective.shape[1]
+    n_rows = row_kind.shape[1]
+    total_cols = n_vars * n_col
+    total_rows = n_rows * n_row
+    row_blocks, col_blocks = n_rows // width, n_vars // width
+    steps = ITERS * chunks
+    part = primal_all.shape[1] * SUB
+
+    def row_peer(d):
+        return lax.rem(r + d, n_row)
+
+    def col_peer(d):
+        return lax.rem(c + d, n_col)
+
+    def row_copy(src, dst, d, out_sem, in_sem):
+        return pltpu.make_async_remote_copy(
+            src_ref=src, dst_ref=dst, send_sem=out_sem, recv_sem=in_sem,
+            device_id={"row": row_peer(d)}, device_id_type=MESH,
+        )
+
+    def col_copy(src, dst, d, out_sem, in_sem):
+        return pltpu.make_async_remote_copy(
+            src_ref=src, dst_ref=dst, send_sem=out_sem, recv_sem=in_sem,
+            device_id={"col": col_peer(d)}, device_id_type=MESH,
+        )
+
+    def row_rs(s, d):
+        k = lax.rem(s, chunks)
+        return row_copy(row_send.at[s, row_peer(d)], row_recv.at[s, d - 1], d,
+                        row_rs_out.at[k, d - 1], row_rs_in.at[k, d - 1])
+
+    def col_rs(s, d):
+        k = lax.rem(s, chunks)
+        return col_copy(col_send.at[s, col_peer(d)], col_recv.at[s, d - 1], d,
+                        col_rs_out.at[k, d - 1], col_rs_in.at[k, d - 1])
+
+    def row_ag(s, d):
+        k = lax.rem(s, chunks)
+        here = primal_all.at[s + chunks, r]
+        return row_copy(here, here, d, row_ag_out.at[k, d - 1], row_ag_in.at[k, d - 1])
+
+    def col_ag(s, d):
+        k = lax.rem(s, chunks)
+        here = dual_all.at[s + chunks, c]
+        return col_copy(here, here, d, col_ag_out.at[k, d - 1], col_ag_in.at[k, d - 1])
+
+    def cost_copy(d):
+        return col_copy(cost_all.at[0], cost_all.at[d], d, cost_out.at[d - 1], cost_in.at[d - 1])
+
+    barrier = pltpu.get_barrier_semaphore()
+    for d in range(1, n_row):
+        pl.semaphore_signal(barrier, inc=1, device_id={"row": row_peer(d)}, device_id_type=MESH)
+    for d in range(1, n_col):
+        pl.semaphore_signal(barrier, inc=1, device_id={"col": col_peer(d)}, device_id_type=MESH)
+
+    costs = objective[...]
+    cost_all[0] = jnp.broadcast_to(jnp.sum(costs * costs, axis=1, keepdims=True), (SUB, LANE))
+
+    for k in range(chunks):
+        rows = pl.ds(k * part, part)
+        shape = (part // SUB, SUB, n_vars)
+        primal_all[k, :, :, :n_vars] = primal_start[rows, :].reshape(shape)
+        primal_all[k, :, :, n_vars:] = jnp.ones((part // SUB, SUB, LANE), jnp.float32)
+        shape = (part // SUB, SUB, n_rows)
+        dual_all[k, :, :, :n_rows] = dual_start[rows, :].reshape(shape)
+        dual_all[k, :, :, n_rows:] = jnp.ones((part // SUB, SUB, LANE), jnp.float32)
+
+    keys = []
+    for t in range(slots):
+        key = spots[t, 0] * col_blocks + spots[t, 1]
+        keys.append(jnp.where(t < counts[0, 0], key, -1))
+    for p in range(row_blocks * col_blocks):
+        slot = jnp.int32(0)
+        live = jnp.float32(0.0)
+        for t in range(slots):
+            hit = keys[t] == p
+            slot = jnp.where(hit, jnp.int32(t), slot)
+            live = jnp.where(hit, jnp.float32(1.0), live)
+        rb, cb = p // col_blocks, p % col_blocks
+        tile = (tiles[slot].astype(jnp.float32) * live).astype(jnp.bfloat16)
+        matrix[rb * width:(rb + 1) * width, cb * width:(cb + 1) * width] = tile
+
+    pl.semaphore_wait(barrier, n_row + n_col - 2)
+    for d in range(1, n_col):
+        cost_copy(d).start()
+
+    def wide(value, width_):
+        return jnp.concatenate([value] * (width_ // LANE), axis=1)
+
+    def gradient_part(s):
+        k = lax.rem(s, chunks)
+        held = dual_all[s, :, :, :n_rows].reshape(part, n_rows)
+        first = dual_all[k, :, :, :n_rows].reshape(part, n_rows)
+        side = right_side[pl.ds(pl.multiple_of(k * part, part), part), :]
+        gap = jnp.where(s < chunks, side, held - first)
+        squares = jnp.sum(gap * gap, axis=1, keepdims=True)
+        terms = jnp.dot(held.astype(jnp.bfloat16), matrix[...], preferred_element_type=jnp.float32)
+        row_send[s, :, :, :n_vars] = terms.reshape(part // SUB, SUB, n_vars)
+        row_send[s, :, :, n_vars:] = jnp.broadcast_to(squares, (part, LANE)).reshape(part // SUB, SUB, LANE)
+        for d in range(1, n_row):
+            row_rs(s, d).start()
+
+    def primal_step(s):
+        for d in range(1, n_row):
+            row_rs(s, d).wait()
+        total = row_send[s, r]
+        for d in range(1, n_row):
+            total = total + row_recv[s, d - 1]
+        gradient, dual_total = total[:, :n_vars], total[:, n_vars:]
+        held = primal_all[s, r]
+        old, old_weight = held[:, :n_vars], held[:, n_vars:]
+        primal_total = dual_all[s, r, :, n_rows:]
+        dual_spread = jnp.sqrt(dual_total / total_rows + EPSILON)
+        scale = jnp.sqrt(cost_total[...] / total_cols + EPSILON)
+        primal_spread = jnp.sqrt(primal_total / total_cols + EPSILON)
+        later = jnp.sqrt(old_weight * dual_spread / primal_spread)
+        weight = jnp.where(s < chunks, scale / dual_spread, later)
+        step = wide(STEP_SCALE / weight, n_vars)
+        low = lower[...]
+        new = old - step * (objective[...] - gradient)
+        new = project_primal(new, low, low + span[...], var_kind[...])
+        primal_all[s + chunks, r, :, :n_vars] = new
+        primal_all[s + chunks, r, :, n_vars:] = weight
+        for d in range(1, n_row):
+            row_ag(s, d).start()
+
+    def image_part(s):
+        k = lax.rem(s, chunks)
+        for d in range(1, n_row):
+            row_ag(s, d).wait()
+        new = primal_all[s + chunks, :, :, :n_vars].reshape(part, n_vars)
+        old = primal_all[s, :, :, :n_vars].reshape(part, n_vars)
+        gap = new - primal_all[k, :, :, :n_vars].reshape(part, n_vars)
+        squares = jnp.sum(gap * gap, axis=1, keepdims=True)
+        ahead = (2.0 * new - old).astype(jnp.bfloat16)
+        terms = jnp.dot(ahead, matrix_t[...], preferred_element_type=jnp.float32)
+        col_send[s, :, :, :n_rows] = terms.reshape(part // SUB, SUB, n_rows)
+        col_send[s, :, :, n_rows:] = jnp.broadcast_to(squares, (part, LANE)).reshape(part // SUB, SUB, LANE)
+        for d in range(1, n_col):
+            col_rs(s, d).start()
+        primal_out[pl.ds(pl.multiple_of(k * part, part), part), :] = new
+
+    def dual_step(s):
+        for d in range(1, n_col):
+            col_rs(s, d).wait()
+        total = col_send[s, c]
+        for d in range(1, n_col):
+            total = total + col_recv[s, d - 1]
+        k = lax.rem(s, chunks)
+        at = k * part + c * SUB
+        side = right_side[pl.ds(pl.multiple_of(at, SUB), SUB), :]
+        step = wide(STEP_SCALE * primal_all[s + chunks, c, :, n_vars:], n_rows)
+        new = dual_all[s, c, :, :n_rows] + step * (side - total[:, :n_rows])
+        new = project_dual(new, row_kind[...])
+        dual_all[s + chunks, c, :, :n_rows] = new
+        dual_all[s + chunks, c, :, n_rows:] = total[:, n_rows:]
+        for d in range(1, n_col):
+            col_ag(s, d).start()
+
+    def dual_arrive(s):
+        for d in range(1, n_col):
+            col_ag(s, d).wait()
+
+        @pl.when(s >= steps - chunks)
+        def _():
+            k = lax.rem(s, chunks)
+            new = dual_all[s + chunks, :, :, :n_rows].reshape(part, n_rows)
+            dual_out[pl.ds(pl.multiple_of(k * part, part), part), :] = new
+
+    def one_step(t, carry):
+        @pl.when(t >= 4)
+        def _():
+            dual_arrive(t - 4)
+
+        @pl.when(t < steps)
+        def _():
+            gradient_part(t)
+
+        @pl.when(t == 0)
+        def _():
+            for rb in range(row_blocks):
+                for cb in range(col_blocks):
+                    tile = matrix[rb * width:(rb + 1) * width, cb * width:(cb + 1) * width]
+                    matrix_t[cb * width:(cb + 1) * width, rb * width:(rb + 1) * width] = tile.T
+            for d in range(1, n_col):
+                cost_copy(d).wait()
+            total = cost_all[0]
+            for d in range(1, n_col):
+                total = total + cost_all[d]
+            cost_total[...] = total
+
+        @pl.when((t >= 3) & (t < steps + 3))
+        def _():
+            dual_step(t - 3)
+
+        @pl.when((t >= 2) & (t < steps + 2))
+        def _():
+            image_part(t - 2)
+
+        @pl.when((t >= 1) & (t < steps + 1))
+        def _():
+            primal_step(t - 1)
+
+        return carry
+
+    lax.fori_loop(0, steps + 4, one_step, 0)
+
+
+def fused(
+    tile_values,
+    tile_spots,
+    tile_counts,
+    objective,
+    lower_bound,
+    bound_span,
+    var_kind,
+    right_side,
+    row_kind,
+    primal_start,
+    dual_start,
+):
+    n_row, n_col = lax.axis_size("row"), lax.axis_size("col")
+    scenarios, n_rows = right_side.shape
+    n_vars = objective.shape[0]
+    owners = n_row
+    chunks = scenarios // (SUB * owners)
+    steps = ITERS * chunks
+    vmem = pl.BlockSpec(memory_space=pltpu.VMEM)
+    smem = pl.BlockSpec(memory_space=pltpu.SMEM)
+    floats = lambda *shape: pltpu.VMEM(shape, jnp.float32)
+    sems = lambda *shape: pltpu.SemaphoreType.DMA(shape)
+    wide_v, wide_r = n_vars + LANE, n_rows + LANE
+    return pl.pallas_call(
+        functools.partial(kernel, n_row, n_col, chunks),
+        out_shape=(
+            jax.ShapeDtypeStruct(primal_start.shape, jnp.float32),
+            jax.ShapeDtypeStruct(dual_start.shape, jnp.float32),
+        ),
+        in_specs=[vmem, smem, smem] + [vmem] * 8,
+        out_specs=(vmem, vmem),
+        scratch_shapes=[
+            pltpu.VMEM((n_rows, n_vars), jnp.bfloat16),
+            pltpu.VMEM((n_vars, n_rows), jnp.bfloat16),
+            floats(steps + chunks, owners, SUB, wide_v),
+            floats(steps + chunks, owners, SUB, wide_r),
+            floats(steps, owners, SUB, wide_v),
+            floats(steps, owners, SUB, wide_r),
+            floats(steps, n_row - 1, SUB, wide_v),
+            floats(steps, n_col - 1, SUB, wide_r),
+            floats(n_col, SUB, LANE),
+            floats(SUB, LANE),
+            sems(chunks, n_row - 1), sems(chunks, n_row - 1),
+            sems(chunks, n_row - 1), sems(chunks, n_row - 1),
+            sems(chunks, n_col - 1), sems(chunks, n_col - 1),
+            sems(chunks, n_col - 1), sems(chunks, n_col - 1),
+            sems(n_col - 1), sems(n_col - 1),
+        ],
+        compiler_params=pltpu.CompilerParams(
+            collective_id=0, has_side_effects=True, vmem_limit_bytes=48 * 2**20
+        ),
+    )(
+        tile_values.reshape(tile_values.shape[2:]),
+        tile_spots.reshape(tile_spots.shape[2:]),
+        tile_counts,
+        objective.reshape(1, -1),
+        lower_bound.reshape(1, -1),
+        bound_span.reshape(1, -1),
+        var_kind.reshape(1, -1),
+        right_side,
+        row_kind.reshape(1, -1),
+        primal_start,
+        dual_start,
+    )
+
+
+def local(*args):
+    n_row, n_col = lax.axis_size("row"), lax.axis_size("col")
+    scenarios = args[7].shape[0]
+    if n_row == n_col and scenarios == SUB * n_row * 4:
+        return fused(*args)
+    return plain(*args)
+
+
 def solution(mesh):
     placed = (
         P(("lp", "row"), "col", None, None, None),

time: 306 us -> 107 us (0.35)
  waiting for transfers between devices: 156 us -> 0 us
  Pallas kernels: 0 us -> 94.4 us
  blocking collectives: 56.4 us -> 0 us
  matrix products: 26.2 us -> 0 us
  local copies, waits for them, and re-layouts: 33.8 us -> 10.5 us
  other arithmetic: 16.3 us -> 0 us
  between operations: 15.9 us -> 1.3 us
    psum x6 -> x0, waiting for transfers between devices: 155 us -> none  [the longest x3 95.7 us: local(): image = lax.psum(partial_image, 'col')]
    pallas_call x0 -> x1, Pallas kernels: none -> 94.4 us  [fused(): pl.pallas_call(functools.partial(kernel, n_row, n_col, chunks), out_shape...]
    psum x6 -> x0, blocking collectives: 56.4 us -> none  [the longest x2 24 us: local(): dual_total = lax.psum(dual_stat, 'row')]
    dot_general x12 -> x0, matrix products: 26.2 us -> none  [the longest x3 8.48 us: primal_product(): jnp.einsum('tr,kti->kri', target, products, precision=lax.Precision.HIGHEST)]
    reshape x12 -> x1, local copies, waits for them, and re-layouts: 14 us -> 0.76 us  [fused(): tile_spots.reshape(tile_spots.shape[2:])]
    gather x6 -> x0, local copies, waits for them, and re-layouts: 8.63 us -> none  [the longest x3 4.81 us: dual_product(): picked = jnp.take(blocks, places[:, 0], axis=1)]
    reduce_sum x6 -> x0, other arithmetic: 8.42 us -> none  [the longest x2 3.93 us: local(): primal_squares = jnp.sum((primal_next - primal_start) ** 2, axis=1)]
    convert_element_type x6 -> x0, other arithmetic: 4.98 us -> none  [the longest x3 4.15 us: local(): extrapolated = (2.0 * primal_next - primal).astype(jnp.bfloat16)]
  transfers between devices with their start and end apart: 6 -> 0, of which waited for: 6 -> 0; matrix products, arithmetic and copies ran while one was open for 2% -> 0% of each run, Pallas kernels for 0% -> 0%
where the time goes in v1:
time: 107 us; the launch traced here: 106 us
  Pallas kernels  94.4 us (88%)
  local copies, waits for them, and re-layouts  10.5 us (10%)
  between operations  1.3 us (1%)
    pallas_call x1, Pallas kernels, fused(): pl.pallas_call(functools.partial(kernel, n_row, n_col, chunks), out_shape...  94.4 us
    unnamed x20, local copies, waits for them, and re-layouts  9.73 us

profile of v1, /device:TPU:0, one launch (start us, length us, event | category | flops | bytes accessed | tf_op | source)
XLA Modules:
  0.0 106.2 jit_solution(8063566452596457859)
XLA Ops:
  1.3 0.8 copy.13.spots
  2.0 0.0 copy-start
  2.0 1.6 %copy-done = bf16[1,1,16,256,256]{4,3,2,1,0:T(8,128)(2,1)S(1)} copy-done((bf16[1,1,16,256,256]{4,3,2,1,0:T(8,128)(2,1)S(1)}, bf16[1,1,16,256,256]{4,3,2,1,0:T(8,128)(2,1)}, u32[]{:S(2)}) %copy-start) | copy-done | bytes 2097176
  3.6 0.0 copy-start.1
  3.6 1.0 copy-done.1
  4.7 0.0 copy-start.2
  4.7 1.0 copy-done.2
  5.7 0.0 copy-start.3
  5.7 1.0 copy-done.3
  6.8 0.0 copy-start.4
  6.8 0.7 copy-done.4
  7.4 0.0 copy-start.5
  7.4 0.7 copy-done.5
  8.1 0.0 copy-start.6
  8.1 0.7 copy-done.6
  8.8 0.0 copy-start.7
  8.8 0.7 copy-done.7
  9.5 0.0 copy-start.8
  9.5 0.7 copy-done.8
  10.2 94.4 %shard_map.122 = (f32[128,1024]{1,0:T(8,128)S(1)}, f32[128,1024]{1,0:T(8,128)S(1)}) custom-call(bf16[16,256,256]{2,1,0:T(8,128)(2,1)S(1)} %bitcast.7, s32[16,2]{1,0:T(8,128)S(1)} %copy.13.spots, s32[1,1]{1,0:T(1,128)S(6)} %copy.16.counts, f32[1,1024]{1,0:T(1,128)S(1)} %bitcast.8, f32[1,1024]{1,0:T(1,128)S(1)} %bitcast.9, f32[1,1024]{1,0:T(1,128)S(1)} %bitcast.10, ...), custom_call_target="tpu_custom_call" | custom-call | tf_op jit(solution)/shard_map/pallas_call | solution.py:392
  104.6 0.8 copy.17
  105.4 0.8 copy.18
Async XLA Ops:
  2.0 1.6 %copy-start = (bf16[1,1,16,256,256]{4,3,2,1,0:T(8,128)(2,1)S(1)}, bf16[1,1,16,256,256]{4,3,2,1,0:T(8,128)(2,1)}, u32[]{:S(2)}) copy-start(bf16[1,1,16,256,256]{4,3,2,1,0:T(8,128)(2,1)} %param.11) | copy-start | bytes 6291460
  3.6 1.0 copy-start.1
  4.7 1.0 copy-start.2
  5.7 1.0 copy-start.3
  6.8 0.7 copy-start.4
  7.4 0.7 copy-start.5
  8.1 0.7 copy-start.6
  8.8 0.7 copy-start.7
  9.5 0.7 copy-start.8

commit v2 on v1

--- a/solution.py
+++ b/solution.py
@@ -10,7 +10,7 @@
 ITERS = 3
 STEP_SCALE = 0.4
 EPSILON = 1e-06
-SUB = 8
+SUB = 4
 LANE = 128
 MESH = pl.DeviceIdType.MESH
 
@@ -120,9 +120,20 @@
     n_row,
     n_col,
     chunks,
-    tiles,
+    tiles_hbm,
     spots,
     counts,
+    objective_hbm,
+    lower_hbm,
+    span_hbm,
+    var_kind_hbm,
+    right_side_hbm,
+    row_kind_hbm,
+    primal_start_hbm,
+    dual_start_hbm,
+    primal_out,
+    dual_out,
+    tiles,
     objective,
     lower,
     span,
@@ -131,14 +142,16 @@
     row_kind,
     primal_start,
     dual_start,
-    primal_out,
-    dual_out,
+    sides,
+    load_sem,
     matrix,
     matrix_t,
     primal_all,
     dual_all,
     row_send,
     col_send,
+    row_mid,
+    row_pass,
     row_recv,
     col_recv,
     cost_all,
@@ -156,6 +169,7 @@
 ):
     r = lax.axis_index("row")
     c = lax.axis_index("col")
+    odd, upper = lax.rem(r, 2), r // 2
     slots, width = tiles.shape[0], tiles.shape[1]
     n_vars = objective.shape[1]
     n_rows = row_kind.shape[1]
@@ -183,10 +197,18 @@
             device_id={"col": col_peer(d)}, device_id_type=MESH,
         )
 
-    def row_rs(s, d):
-        k = lax.rem(s, chunks)
-        return row_copy(row_send.at[s, row_peer(d)], row_recv.at[s, d - 1], d,
-                        row_rs_out.at[k, d - 1], row_rs_in.at[k, d - 1])
+    def pair_rs(s):
+        k = lax.rem(s, chunks)
+        return pltpu.make_async_remote_copy(
+            src_ref=row_send.at[s, 1 - odd], dst_ref=row_mid.at[s],
+            send_sem=row_rs_out.at[k, 0], recv_sem=row_rs_in.at[k, 0],
+            device_id={"row": r + 1 - 2 * odd}, device_id_type=MESH,
+        )
+
+    def half_rs(s):
+        k = lax.rem(s, chunks)
+        return row_copy(row_pass.at[s], row_recv.at[s], n_row // 2,
+                        row_rs_out.at[k, 1], row_rs_in.at[k, 1])
 
     def col_rs(s, d):
         k = lax.rem(s, chunks)
@@ -205,6 +227,21 @@
 
     def cost_copy(d):
         return col_copy(cost_all.at[0], cost_all.at[d], d, cost_out.at[d - 1], cost_in.at[d - 1])
+
+    loads = [
+        (tiles_hbm, tiles),
+        (dual_start_hbm, dual_start),
+        (right_side_hbm, right_side),
+        (objective_hbm, objective),
+        (primal_start_hbm, primal_start),
+        (lower_hbm, lower),
+        (span_hbm, span),
+        (var_kind_hbm, var_kind),
+        (row_kind_hbm, row_kind),
+    ]
+    loads = [pltpu.make_async_copy(src, dst, load_sem.at[i]) for i, (src, dst) in enumerate(loads)]
+    for load in loads:
+        load.start()
 
     barrier = pltpu.get_barrier_semaphore()
     for d in range(1, n_row):
@@ -212,22 +249,15 @@
     for d in range(1, n_col):
         pl.semaphore_signal(barrier, inc=1, device_id={"col": col_peer(d)}, device_id_type=MESH)
 
-    costs = objective[...]
-    cost_all[0] = jnp.broadcast_to(jnp.sum(costs * costs, axis=1, keepdims=True), (SUB, LANE))
-
     for k in range(chunks):
-        rows = pl.ds(k * part, part)
-        shape = (part // SUB, SUB, n_vars)
-        primal_all[k, :, :, :n_vars] = primal_start[rows, :].reshape(shape)
         primal_all[k, :, :, n_vars:] = jnp.ones((part // SUB, SUB, LANE), jnp.float32)
-        shape = (part // SUB, SUB, n_rows)
-        dual_all[k, :, :, :n_rows] = dual_start[rows, :].reshape(shape)
         dual_all[k, :, :, n_rows:] = jnp.ones((part // SUB, SUB, LANE), jnp.float32)
 
     keys = []
     for t in range(slots):
         key = spots[t, 0] * col_blocks + spots[t, 1]
         keys.append(jnp.where(t < counts[0, 0], key, -1))
+    loads[0].wait()
     for p in range(row_blocks * col_blocks):
         slot = jnp.int32(0)
         live = jnp.float32(0.0)
@@ -239,6 +269,17 @@
         tile = (tiles[slot].astype(jnp.float32) * live).astype(jnp.bfloat16)
         matrix[rb * width:(rb + 1) * width, cb * width:(cb + 1) * width] = tile
 
+    for load in loads[1:]:
+        load.wait()
+    costs = objective[...]
+    cost_all[0] = jnp.broadcast_to(jnp.sum(costs * costs, axis=1, keepdims=True), (SUB, LANE))
+
+    for k in range(chunks):
+        for q in range(n_row):
+            rows = slice(k * part + q * SUB, k * part + (q + 1) * SUB)
+            primal_all[k, q, :, :n_vars] = primal_start[rows, :]
+            dual_all[k, q, :, :n_rows] = dual_start[rows, :]
+            sides[k, q] = right_side[rows, :]
     pl.semaphore_wait(barrier, n_row + n_col - 2)
     for d in range(1, n_col):
         cost_copy(d).start()
@@ -246,25 +287,28 @@
     def wide(value, width_):
         return jnp.concatenate([value] * (width_ // LANE), axis=1)
 
+    def stacked(value):
+        return jnp.concatenate([value[q] for q in range(value.shape[0])], axis=0)
+
     def gradient_part(s):
         k = lax.rem(s, chunks)
-        held = dual_all[s, :, :, :n_rows].reshape(part, n_rows)
-        first = dual_all[k, :, :, :n_rows].reshape(part, n_rows)
-        side = right_side[pl.ds(pl.multiple_of(k * part, part), part), :]
-        gap = jnp.where(s < chunks, side, held - first)
-        squares = jnp.sum(gap * gap, axis=1, keepdims=True)
-        terms = jnp.dot(held.astype(jnp.bfloat16), matrix[...], preferred_element_type=jnp.float32)
-        row_send[s, :, :, :n_vars] = terms.reshape(part // SUB, SUB, n_vars)
-        row_send[s, :, :, n_vars:] = jnp.broadcast_to(squares, (part, LANE)).reshape(part // SUB, SUB, LANE)
-        for d in range(1, n_row):
-            row_rs(s, d).start()
+        held = dual_all[s, :, :, :n_rows]
+        gap = jnp.where(s < chunks, sides[k], held - dual_all[k, :, :, :n_rows])
+        spread = jnp.broadcast_to(jnp.sum(gap * gap, axis=2, keepdims=True), (n_row, SUB, LANE))
+        terms = jnp.dot(stacked(held).astype(jnp.bfloat16), matrix[...], preferred_element_type=jnp.float32)
+        for q in range(n_row):
+            row_send[s, q % 2, q // 2, :, :n_vars] = terms[q * SUB:(q + 1) * SUB]
+            row_send[s, q % 2, q // 2, :, n_vars:] = spread[q]
+        pair_rs(s).start()
+
+    def pass_on(s):
+        pair_rs(s).wait()
+        row_pass[s] = row_send[s, odd, 1 - upper] + row_mid[s, 1 - upper]
+        half_rs(s).start()
 
     def primal_step(s):
-        for d in range(1, n_row):
-            row_rs(s, d).wait()
-        total = row_send[s, r]
-        for d in range(1, n_row):
-            total = total + row_recv[s, d - 1]
+        half_rs(s).wait()
+        total = row_send[s, odd, upper] + row_mid[s, upper] + row_recv[s]
         gradient, dual_total = total[:, :n_vars], total[:, n_vars:]
         held = primal_all[s, r]
         old, old_weight = held[:, :n_vars], held[:, n_vars:]
@@ -287,17 +331,21 @@
         k = lax.rem(s, chunks)
         for d in range(1, n_row):
             row_ag(s, d).wait()
-        new = primal_all[s + chunks, :, :, :n_vars].reshape(part, n_vars)
-        old = primal_all[s, :, :, :n_vars].reshape(part, n_vars)
-        gap = new - primal_all[k, :, :, :n_vars].reshape(part, n_vars)
-        squares = jnp.sum(gap * gap, axis=1, keepdims=True)
-        ahead = (2.0 * new - old).astype(jnp.bfloat16)
+        new = primal_all[s + chunks, :, :, :n_vars]
+        old = primal_all[s, :, :, :n_vars]
+        gap = new - primal_all[k, :, :, :n_vars]
+        spread = jnp.broadcast_to(jnp.sum(gap * gap, axis=2, keepdims=True), (n_row, SUB, LANE))
+        ahead = stacked(2.0 * new - old).astype(jnp.bfloat16)
         terms = jnp.dot(ahead, matrix_t[...], preferred_element_type=jnp.float32)
-        col_send[s, :, :, :n_rows] = terms.reshape(part // SUB, SUB, n_rows)
-        col_send[s, :, :, n_rows:] = jnp.broadcast_to(squares, (part, LANE)).reshape(part // SUB, SUB, LANE)
+        for q in range(n_col):
+            col_send[s, q, :, :n_rows] = terms[q * SUB:(q + 1) * SUB]
+            col_send[s, q, :, n_rows:] = spread[q]
         for d in range(1, n_col):
             col_rs(s, d).start()
-        primal_out[pl.ds(pl.multiple_of(k * part, part), part), :] = new
+
+        @pl.when(s >= steps - chunks)
+        def _():
+            primal_out[pl.ds(pl.multiple_of(k * part, part), part), :] = stacked(new)
 
     def dual_step(s):
         for d in range(1, n_col):
@@ -306,8 +354,7 @@
         for d in range(1, n_col):
             total = total + col_recv[s, d - 1]
         k = lax.rem(s, chunks)
-        at = k * part + c * SUB
-        side = right_side[pl.ds(pl.multiple_of(at, SUB), SUB), :]
+        side = sides[k, c]
         step = wide(STEP_SCALE * primal_all[s + chunks, c, :, n_vars:], n_rows)
         new = dual_all[s, c, :, :n_rows] + step * (side - total[:, :n_rows])
         new = project_dual(new, row_kind[...])
@@ -323,17 +370,17 @@
         @pl.when(s >= steps - chunks)
         def _():
             k = lax.rem(s, chunks)
-            new = dual_all[s + chunks, :, :, :n_rows].reshape(part, n_rows)
+            new = stacked(dual_all[s + chunks, :, :, :n_rows])
             dual_out[pl.ds(pl.multiple_of(k * part, part), part), :] = new
 
     def one_step(t, carry):
-        @pl.when(t >= 4)
-        def _():
-            dual_arrive(t - 4)
-
-        @pl.when(t < steps)
-        def _():
-            gradient_part(t)
+        def stage(delay, run):
+            @pl.when((t >= delay) & (t < steps + delay))
+            def _():
+                run(t - delay)
+
+        stage(chunks, dual_arrive)
+        stage(0, gradient_part)
 
         @pl.when(t == 0)
         def _():
@@ -348,21 +395,13 @@
                 total = total + cost_all[d]
             cost_total[...] = total
 
-        @pl.when((t >= 3) & (t < steps + 3))
-        def _():
-            dual_step(t - 3)
-
-        @pl.when((t >= 2) & (t < steps + 2))
-        def _():
-            image_part(t - 2)
-
-        @pl.when((t >= 1) & (t < steps + 1))
-        def _():
-            primal_step(t - 1)
-
+        stage(3, primal_step)
+        stage(6, dual_step)
+        stage(1, pass_on)
+        stage(4, image_part)
         return carry
 
-    lax.fori_loop(0, steps + 4, one_step, 0)
+    lax.fori_loop(0, steps + chunks, one_step, 0)
 
 
 def fused(
@@ -386,6 +425,7 @@
     steps = ITERS * chunks
     vmem = pl.BlockSpec(memory_space=pltpu.VMEM)
     smem = pl.BlockSpec(memory_space=pltpu.SMEM)
+    hbm = pl.BlockSpec(memory_space=pltpu.HBM)
     floats = lambda *shape: pltpu.VMEM(shape, jnp.float32)
     sems = lambda *shape: pltpu.SemaphoreType.DMA(shape)
     wide_v, wide_r = n_vars + LANE, n_rows + LANE
@@ -395,27 +435,40 @@
             jax.ShapeDtypeStruct(primal_start.shape, jnp.float32),
             jax.ShapeDtypeStruct(dual_start.shape, jnp.float32),
         ),
-        in_specs=[vmem, smem, smem] + [vmem] * 8,
+        in_specs=[hbm, smem, smem] + [hbm] * 8,
         out_specs=(vmem, vmem),
         scratch_shapes=[
+            pltpu.VMEM(tile_values.shape[2:], jnp.bfloat16),
+            floats(1, n_vars),
+            floats(1, n_vars),
+            floats(1, n_vars),
+            pltpu.VMEM((1, n_vars), jnp.int32),
+            floats(*right_side.shape),
+            pltpu.VMEM((1, n_rows), jnp.int32),
+            floats(*primal_start.shape),
+            floats(*dual_start.shape),
+            floats(chunks, owners, SUB, n_rows),
+            sems(9),
             pltpu.VMEM((n_rows, n_vars), jnp.bfloat16),
             pltpu.VMEM((n_vars, n_rows), jnp.bfloat16),
             floats(steps + chunks, owners, SUB, wide_v),
             floats(steps + chunks, owners, SUB, wide_r),
-            floats(steps, owners, SUB, wide_v),
+            floats(steps, 2, n_row // 2, SUB, wide_v),
             floats(steps, owners, SUB, wide_r),
-            floats(steps, n_row - 1, SUB, wide_v),
+            floats(steps, n_row // 2, SUB, wide_v),
+            floats(steps, SUB, wide_v),
+            floats(steps, SUB, wide_v),
             floats(steps, n_col - 1, SUB, wide_r),
             floats(n_col, SUB, LANE),
             floats(SUB, LANE),
-            sems(chunks, n_row - 1), sems(chunks, n_row - 1),
+            sems(chunks, 2), sems(chunks, 2),
             sems(chunks, n_row - 1), sems(chunks, n_row - 1),
             sems(chunks, n_col - 1), sems(chunks, n_col - 1),
             sems(chunks, n_col - 1), sems(chunks, n_col - 1),
             sems(n_col - 1), sems(n_col - 1),
         ],
         compiler_params=pltpu.CompilerParams(
-            collective_id=0, has_side_effects=True, vmem_limit_bytes=48 * 2**20
+            collective_id=0, has_side_effects=True, vmem_limit_bytes=60 * 2**20
         ),
     )(
         tile_values.reshape(tile_values.shape[2:]),
@@ -435,7 +488,7 @@
 def local(*args):
     n_row, n_col = lax.axis_size("row"), lax.axis_size("col")
     scenarios = args[7].shape[0]
-    if n_row == n_col and scenarios == SUB * n_row * 4:
+    if n_row == n_col and scenarios == SUB * n_row * 8:
         return fused(*args)
     return plain(*args)
 

time: 107 us -> 95.7 us (0.89)
  Pallas kernels: 94.4 us -> 89 us
  local copies, waits for them, and re-layouts: 10.5 us -> 5.12 us
    unnamed x20 -> x2, local copies, waits for them, and re-layouts: 9.73 us -> 3.77 us
    pallas_call x1, Pallas kernels: 94.4 us -> 89 us  [fused(): pl.pallas_call(functools.partial(kernel, n_row, n_col, chunks), out_shape...]
where the time goes in v2:
time: 95.7 us; the launch traced here: 95.4 us
  Pallas kernels  89 us (93%)
  local copies, waits for them, and re-layouts  5.12 us (5%)
  between operations  1.29 us (1%)
    pallas_call x1, Pallas kernels, fused(): pl.pallas_call(functools.partial(kernel, n_row, n_col, chunks), out_shape...  89 us
    unnamed x2, local copies, waits for them, and re-layouts  3.77 us

profile of v2, /device:TPU:0, one launch (start us, length us, event | category | flops | bytes accessed | tf_op | source)
XLA Modules:
  0.0 95.4 jit_solution(5523304929285371307)
XLA Ops:
  1.3 1.4 %copy.13.spots = s32[16,2]{1,0:T(8,128)} copy(s32[16,2]{0,1:T(2,128)} %bitcast.13) | data formatting | bytes 256 | tf_op jit(solution)/shard_map/reshape | solution.py:475
  2.6 89.0 %shard_map.122 = (f32[128,1024]{1,0:T(8,128)}, f32[128,1024]{1,0:T(8,128)}) custom-call(bf16[16,256,256]{2,1,0:T(8,128)(2,1)} %bitcast.7, s32[16,2]{1,0:T(8,128)} %copy.13.spots, s32[1,1]{1,0:T(1,128)S(6)} %copy.16.counts, f32[1,1024]{1,0:T(1,128)} %bitcast.8, f32[1,1024]{1,0:T(1,128)} %bitcast.9, f32[1,1024]{1,0:T(1,128)} %bitcast.10, s32[1,1024]{1,0:T(1,128)} %bitcast.11, ...), custom_call_target="tpu_custom_call" | custom-call | tf_op jit(solution)/shard_map/pallas_call | solution.py:432
  91.6 1.9 %copy.17 = f32[128,1024]{1,0:T(8,128)} copy(f32[128,1024]{1,0:T(8,128)} %get-tuple-element.4) | data formatting | bytes 1048576
  93.5 1.9 %copy.18 = f32[128,1024]{1,0:T(8,128)} copy(f32[128,1024]{1,0:T(8,128)} %get-tuple-element.5) | data formatting | bytes 1048576

commit v3 on v2

--- a/solution.py
+++ b/solution.py
@@ -156,13 +156,10 @@
     col_recv,
     cost_all,
     cost_total,
-    row_rs_out,
+    sent,
     row_rs_in,
-    row_ag_out,
     row_ag_in,
-    col_rs_out,
     col_rs_in,
-    col_ag_out,
     col_ag_in,
     cost_out,
     cost_in,
@@ -201,29 +198,35 @@
         k = lax.rem(s, chunks)
         return pltpu.make_async_remote_copy(
             src_ref=row_send.at[s, 1 - odd], dst_ref=row_mid.at[s],
-            send_sem=row_rs_out.at[k, 0], recv_sem=row_rs_in.at[k, 0],
+            send_sem=sent.at[0], recv_sem=row_rs_in.at[k, 0],
             device_id={"row": r + 1 - 2 * odd}, device_id_type=MESH,
         )
 
     def half_rs(s):
         k = lax.rem(s, chunks)
         return row_copy(row_pass.at[s], row_recv.at[s], n_row // 2,
-                        row_rs_out.at[k, 1], row_rs_in.at[k, 1])
+                        sent.at[1], row_rs_in.at[k, 1])
 
     def col_rs(s, d):
         k = lax.rem(s, chunks)
         return col_copy(col_send.at[s, col_peer(d)], col_recv.at[s, d - 1], d,
-                        col_rs_out.at[k, d - 1], col_rs_in.at[k, d - 1])
+                        sent.at[3], col_rs_in.at[k])
 
     def row_ag(s, d):
         k = lax.rem(s, chunks)
         here = primal_all.at[s + chunks, r]
-        return row_copy(here, here, d, row_ag_out.at[k, d - 1], row_ag_in.at[k, d - 1])
+        return row_copy(here, here, d, sent.at[2], row_ag_in.at[k])
 
     def col_ag(s, d):
         k = lax.rem(s, chunks)
         here = dual_all.at[s + chunks, c]
-        return col_copy(here, here, d, col_ag_out.at[k, d - 1], col_ag_in.at[k, d - 1])
+        return col_copy(here, here, d, sent.at[4], col_ag_in.at[k])
+
+    def bytes_of(ref, sem):
+        pltpu.make_async_copy(ref, ref, sem).wait()
+
+    def arrived(sem):
+        bytes_of(col_recv.at[0], sem)
 
     def cost_copy(d):
         return col_copy(cost_all.at[0], cost_all.at[d], d, cost_out.at[d - 1], cost_in.at[d - 1])
@@ -302,12 +305,12 @@
         pair_rs(s).start()
 
     def pass_on(s):
-        pair_rs(s).wait()
+        pair_rs(s).wait_recv()
         row_pass[s] = row_send[s, odd, 1 - upper] + row_mid[s, 1 - upper]
         half_rs(s).start()
 
     def primal_step(s):
-        half_rs(s).wait()
+        half_rs(s).wait_recv()
         total = row_send[s, odd, upper] + row_mid[s, upper] + row_recv[s]
         gradient, dual_total = total[:, :n_vars], total[:, n_vars:]
         held = primal_all[s, r]
@@ -329,8 +332,7 @@
 
     def image_part(s):
         k = lax.rem(s, chunks)
-        for d in range(1, n_row):
-            row_ag(s, d).wait()
+        arrived(row_ag_in.at[k])
         new = primal_all[s + chunks, :, :, :n_vars]
         old = primal_all[s, :, :, :n_vars]
         gap = new - primal_all[k, :, :, :n_vars]
@@ -348,12 +350,11 @@
             primal_out[pl.ds(pl.multiple_of(k * part, part), part), :] = stacked(new)
 
     def dual_step(s):
-        for d in range(1, n_col):
-            col_rs(s, d).wait()
+        k = lax.rem(s, chunks)
+        arrived(col_rs_in.at[k])
         total = col_send[s, c]
         for d in range(1, n_col):
             total = total + col_recv[s, d - 1]
-        k = lax.rem(s, chunks)
         side = sides[k, c]
         step = wide(STEP_SCALE * primal_all[s + chunks, c, :, n_vars:], n_rows)
         new = dual_all[s, c, :, :n_rows] + step * (side - total[:, :n_rows])
@@ -364,8 +365,7 @@
             col_ag(s, d).start()
 
     def dual_arrive(s):
-        for d in range(1, n_col):
-            col_ag(s, d).wait()
+        arrived(col_ag_in.at[lax.rem(s, chunks)])
 
         @pl.when(s >= steps - chunks)
         def _():
@@ -395,13 +395,15 @@
                 total = total + cost_all[d]
             cost_total[...] = total
 
+        stage(5, image_part)
         stage(3, primal_step)
+        stage(1, pass_on)
         stage(6, dual_step)
-        stage(1, pass_on)
-        stage(4, image_part)
         return carry
 
     lax.fori_loop(0, steps + chunks, one_step, 0)
+    for i, ref in enumerate([row_mid, row_pass, col_recv, col_recv, col_recv]):
+        bytes_of(ref, sent.at[i])
 
 
 def fused(
@@ -461,10 +463,11 @@
             floats(steps, n_col - 1, SUB, wide_r),
             floats(n_col, SUB, LANE),
             floats(SUB, LANE),
-            sems(chunks, 2), sems(chunks, 2),
-            sems(chunks, n_row - 1), sems(chunks, n_row - 1),
-            sems(chunks, n_col - 1), sems(chunks, n_col - 1),
-            sems(chunks, n_col - 1), sems(chunks, n_col - 1),
+            sems(5),
+            sems(chunks, 2),
+            sems(chunks),
+            sems(chunks),
+            sems(chunks),
             sems(n_col - 1), sems(n_col - 1),
         ],
         compiler_params=pltpu.CompilerParams(
@@ -488,7 +491,8 @@
 def local(*args):
     n_row, n_col = lax.axis_size("row"), lax.axis_size("col")
     scenarios = args[7].shape[0]
-    if n_row == n_col and scenarios == SUB * n_row * 8:
+    square = n_row == n_col and args[3].shape[0] == args[7].shape[1]
+    if square and n_row == 4 and scenarios == SUB * n_row * 8:
         return fused(*args)
     return plain(*args)
 

time: 95.7 us -> 86.7 us (0.906)
  Pallas kernels: 89 us -> 80 us
    pallas_call x1, Pallas kernels: 89 us -> 80 us  [fused(): pl.pallas_call(functools.partial(kernel, n_row, n_col, chunks), out_shape...]
where the time goes in v3:
time: 86.7 us; the launch traced here: 86.5 us
  Pallas kernels  80 us (92%)
  local copies, waits for them, and re-layouts  5.12 us (6%)
  between operations  1.29 us (1%)
    pallas_call x1, Pallas kernels, fused(): pl.pallas_call(functools.partial(kernel, n_row, n_col, chunks), out_shape...  80 us
    unnamed x2, local copies, waits for them, and re-layouts  3.77 us

profile of v3, /device:TPU:0, one launch (start us, length us, event | category | flops | bytes accessed | tf_op | source)
XLA Modules:
  0.0 86.5 jit_solution(10197953073281759487)
XLA Ops:
  1.3 1.4 %copy.13.spots = s32[16,2]{1,0:T(8,128)} copy(s32[16,2]{0,1:T(2,128)} %bitcast.13) | data formatting | bytes 256 | tf_op jit(solution)/shard_map/reshape | solution.py:478
  2.6 80.0 %shard_map.122 = (f32[128,1024]{1,0:T(8,128)}, f32[128,1024]{1,0:T(8,128)}) custom-call(bf16[16,256,256]{2,1,0:T(8,128)(2,1)} %bitcast.7, s32[16,2]{1,0:T(8,128)} %copy.13.spots, s32[1,1]{1,0:T(1,128)S(6)} %copy.16.counts, f32[1,1024]{1,0:T(1,128)} %bitcast.8, f32[1,1024]{1,0:T(1,128)} %bitcast.9, f32[1,1024]{1,0:T(1,128)} %bitcast.10, s32[1,1024]{1,0:T(1,128)} %bitcast.11, ...), custom_call_target="tpu_custom_call" | custom-call | tf_op jit(solution)/shard_map/pallas_call | solution.py:434
  82.7 1.9 %copy.17 = f32[128,1024]{1,0:T(8,128)} copy(f32[128,1024]{1,0:T(8,128)} %get-tuple-element.4) | data formatting | bytes 1048576
  84.6 1.9 %copy.18 = f32[128,1024]{1,0:T(8,128)} copy(f32[128,1024]{1,0:T(8,128)} %get-tuple-element.5) | data formatting | bytes 1048576

commit v4 on v3

--- a/solution.py
+++ b/solution.py
@@ -157,6 +157,7 @@
     cost_all,
     cost_total,
     sent,
+    weight_in,
     row_rs_in,
     row_ag_in,
     col_rs_in,
@@ -214,8 +215,12 @@
 
     def row_ag(s, d):
         k = lax.rem(s, chunks)
-        here = primal_all.at[s + chunks, r]
+        here = primal_all.at[s + chunks, r, :, pl.ds(0, n_vars)]
         return row_copy(here, here, d, sent.at[2], row_ag_in.at[k])
+
+    def weight_copy(s, d):
+        here = primal_all.at[s + chunks, r, :, pl.ds(n_vars, LANE)]
+        return row_copy(here, here, d, sent.at[5], weight_in.at[lax.rem(s, chunks)])
 
     def col_ag(s, d):
         k = lax.rem(s, chunks)
@@ -252,22 +257,17 @@
     for d in range(1, n_col):
         pl.semaphore_signal(barrier, inc=1, device_id={"col": col_peer(d)}, device_id_type=MESH)
 
-    for k in range(chunks):
-        primal_all[k, :, :, n_vars:] = jnp.ones((part // SUB, SUB, LANE), jnp.float32)
-        dual_all[k, :, :, n_rows:] = jnp.ones((part // SUB, SUB, LANE), jnp.float32)
-
     keys = []
     for t in range(slots):
         key = spots[t, 0] * col_blocks + spots[t, 1]
         keys.append(jnp.where(t < counts[0, 0], key, -1))
     loads[0].wait()
     for p in range(row_blocks * col_blocks):
-        slot = jnp.int32(0)
-        live = jnp.float32(0.0)
+        found = jnp.int32(0)
         for t in range(slots):
-            hit = keys[t] == p
-            slot = jnp.where(hit, jnp.int32(t), slot)
-            live = jnp.where(hit, jnp.float32(1.0), live)
+            found = jnp.where(keys[t] == p, jnp.int32(t + 1), found)
+        live = jnp.where(found > 0, jnp.float32(1.0), jnp.float32(0.0))
+        slot = jnp.maximum(found - 1, 0)
         rb, cb = p // col_blocks, p % col_blocks
         tile = (tiles[slot].astype(jnp.float32) * live).astype(jnp.bfloat16)
         matrix[rb * width:(rb + 1) * width, cb * width:(cb + 1) * width] = tile
@@ -277,12 +277,6 @@
     costs = objective[...]
     cost_all[0] = jnp.broadcast_to(jnp.sum(costs * costs, axis=1, keepdims=True), (SUB, LANE))
 
-    for k in range(chunks):
-        for q in range(n_row):
-            rows = slice(k * part + q * SUB, k * part + (q + 1) * SUB)
-            primal_all[k, q, :, :n_vars] = primal_start[rows, :]
-            dual_all[k, q, :, :n_rows] = dual_start[rows, :]
-            sides[k, q] = right_side[rows, :]
     pl.semaphore_wait(barrier, n_row + n_col - 2)
     for d in range(1, n_col):
         cost_copy(d).start()
@@ -330,9 +324,14 @@
         for d in range(1, n_row):
             row_ag(s, d).start()
 
+        @pl.when(r == c)
+        def _():
+            for d in range(1, n_row):
+                weight_copy(s, d).start()
+
     def image_part(s):
         k = lax.rem(s, chunks)
-        arrived(row_ag_in.at[k])
+        bytes_of(col_recv.at[0, :, :, pl.ds(0, n_vars)], row_ag_in.at[k])
         new = primal_all[s + chunks, :, :, :n_vars]
         old = primal_all[s, :, :, :n_vars]
         gap = new - primal_all[k, :, :, :n_vars]
@@ -352,6 +351,11 @@
     def dual_step(s):
         k = lax.rem(s, chunks)
         arrived(col_rs_in.at[k])
+
+        @pl.when(r != c)
+        def _():
+            bytes_of(primal_all.at[s + chunks, c, :, pl.ds(n_vars, LANE)], weight_in.at[k])
+
         total = col_send[s, c]
         for d in range(1, n_col):
             total = total + col_recv[s, d - 1]
@@ -379,10 +383,22 @@
             def _():
                 run(t - delay)
 
+        @pl.when(t < chunks)
+        def _():
+            rows = pl.ds(pl.multiple_of(t * part, part), part)
+            primal, dual, side = primal_start[rows, :], dual_start[rows, :], right_side[rows, :]
+            for q in range(n_row):
+                own = slice(q * SUB, (q + 1) * SUB)
+                primal_all[t, q, :, :n_vars] = primal[own]
+                dual_all[t, q, :, :n_rows] = dual[own]
+                sides[t, q] = side[own]
+            primal_all[t, :, :, n_vars:] = jnp.ones((n_row, SUB, LANE), jnp.float32)
+            dual_all[t, :, :, n_rows:] = jnp.ones((n_col, SUB, LANE), jnp.float32)
+
         stage(chunks, dual_arrive)
         stage(0, gradient_part)
 
-        @pl.when(t == 0)
+        @pl.when(t == 1)
         def _():
             for rb in range(row_blocks):
                 for cb in range(col_blocks):
@@ -402,8 +418,12 @@
         return carry
 
     lax.fori_loop(0, steps + chunks, one_step, 0)
-    for i, ref in enumerate([row_mid, row_pass, col_recv, col_recv, col_recv]):
+    for i, ref in enumerate([row_mid, row_pass, col_recv.at[:, :, :, pl.ds(0, n_vars)], col_recv, col_recv]):
         bytes_of(ref, sent.at[i])
+
+    @pl.when(r == c)
+    def _():
+        bytes_of(col_recv.at[:, :, :, pl.ds(0, LANE)], sent.at[5])
 
 
 def fused(
@@ -463,7 +483,8 @@
             floats(steps, n_col - 1, SUB, wide_r),
             floats(n_col, SUB, LANE),
             floats(SUB, LANE),
-            sems(5),
+            sems(6),
+            sems(chunks),
             sems(chunks, 2),
             sems(chunks),
             sems(chunks),

time: 86.7 us -> 84.4 us (0.973)
  Pallas kernels: 80 us -> 77.7 us
    pallas_call x1, Pallas kernels: 80 us -> 77.7 us  [fused(): pl.pallas_call(functools.partial(kernel, n_row, n_col, chunks), out_shape...]
where the time goes in v4:
time: 84.4 us; the launch traced here: 84.1 us
  Pallas kernels  77.7 us (92%)
  local copies, waits for them, and re-layouts  5.12 us (6%)
  between operations  1.29 us (2%)
    pallas_call x1, Pallas kernels, fused(): pl.pallas_call(functools.partial(kernel, n_row, n_col, chunks), out_shape...  77.7 us
    unnamed x2, local copies, waits for them, and re-layouts  3.77 us

profile of v4, /device:TPU:0, one launch (start us, length us, event | category | flops | bytes accessed | tf_op | source)
XLA Modules:
  0.0 84.1 jit_solution(1275902679357940419)
XLA Ops:
  1.3 1.4 %copy.13.spots = s32[16,2]{1,0:T(8,128)} copy(s32[16,2]{0,1:T(2,128)} %bitcast.13) | data formatting | bytes 256 | tf_op jit(solution)/shard_map/reshape | solution.py:499
  2.6 77.7 %shard_map.122 = (f32[128,1024]{1,0:T(8,128)}, f32[128,1024]{1,0:T(8,128)}) custom-call(bf16[16,256,256]{2,1,0:T(8,128)(2,1)} %bitcast.7, s32[16,2]{1,0:T(8,128)} %copy.13.spots, s32[1,1]{1,0:T(1,128)S(6)} %copy.16.counts, f32[1,1024]{1,0:T(1,128)} %bitcast.8, f32[1,1024]{1,0:T(1,128)} %bitcast.9, f32[1,1024]{1,0:T(1,128)} %bitcast.10, s32[1,1024]{1,0:T(1,128)} %bitcast.11, ...), custom_call_target="tpu_custom_call" | custom-call | tf_op jit(solution)/shard_map/pallas_call | solution.py:454
  80.3 1.9 %copy.17 = f32[128,1024]{1,0:T(8,128)} copy(f32[128,1024]{1,0:T(8,128)} %get-tuple-element.4) | data formatting | bytes 1048576
  82.2 1.9 %copy.18 = f32[128,1024]{1,0:T(8,128)} copy(f32[128,1024]{1,0:T(8,128)} %get-tuple-element.5) | data formatting | bytes 1048576

commit v5 on v4

--- a/solution.py
+++ b/solution.py
@@ -322,7 +322,7 @@
         primal_all[s + chunks, r, :, :n_vars] = new
         primal_all[s + chunks, r, :, n_vars:] = weight
         for d in range(1, n_row):
-            row_ag(s, d).start()
+            row_ag(s, jnp.where(upper == 0, n_row - d, d)).start()
 
         @pl.when(r == c)
         def _():

time: 84.4 us -> 85.2 us (level)
  no operation moved by 1% of the time
where the time goes in v5:
time: 85.2 us; the launch traced here: 84.9 us
  Pallas kernels  78.5 us (92%)
  local copies, waits for them, and re-layouts  5.12 us (6%)
  between operations  1.29 us (2%)
    pallas_call x1, Pallas kernels, fused(): pl.pallas_call(functools.partial(kernel, n_row, n_col, chunks), out_shape...  78.5 us
    unnamed x2, local copies, waits for them, and re-layouts  3.77 us

profile of v5, /device:TPU:0, one launch (start us, length us, event | category | flops | bytes accessed | tf_op | source)
XLA Modules:
  0.0 84.9 jit_solution(1008289352411962938)
XLA Ops:
  1.3 1.4 %copy.13.spots = s32[16,2]{1,0:T(8,128)} copy(s32[16,2]{0,1:T(2,128)} %bitcast.13) | data formatting | bytes 256 | tf_op jit(solution)/shard_map/reshape | solution.py:499
  2.6 78.5 %shard_map.122 = (f32[128,1024]{1,0:T(8,128)}, f32[128,1024]{1,0:T(8,128)}) custom-call(bf16[16,256,256]{2,1,0:T(8,128)(2,1)} %bitcast.7, s32[16,2]{1,0:T(8,128)} %copy.13.spots, s32[1,1]{1,0:T(1,128)S(6)} %copy.16.counts, f32[1,1024]{1,0:T(1,128)} %bitcast.8, f32[1,1024]{1,0:T(1,128)} %bitcast.9, f32[1,1024]{1,0:T(1,128)} %bitcast.10, s32[1,1024]{1,0:T(1,128)} %bitcast.11, ...), custom_call_target="tpu_custom_call" | custom-call | tf_op jit(solution)/shard_map/pallas_call | solution.py:454
  81.1 1.9 %copy.17 = f32[128,1024]{1,0:T(8,128)} copy(f32[128,1024]{1,0:T(8,128)} %get-tuple-element.4) | data formatting | bytes 1048576
  83.0 1.9 %copy.18 = f32[128,1024]{1,0:T(8,128)} copy(f32[128,1024]{1,0:T(8,128)} %get-tuple-element.5) | data formatting | bytes 1048576
